TPU v7x, 512 devices: a whole 4x8x8 slice. The times are simulated.
512 devices in a mesh: layer: 8 (over z), tile: 64 (over x, y, core).
Axes of the slice: x: 4, y: 8, z: 8, core: 2. Of those that a mesh axis runs over, the one named last changes fastest.
Arguments:
- incident: bfloat16 [2, 32768, 128], P(None, 'tile'), may hold values from -6 to 6
- sources: bfloat16 [8, 2, 32768, 128], P('layer', None, 'tile'), may hold values from -6 to 6
- green_tiles: bfloat16 [8, 768, 2, 256, 256], P('layer', 'tile'), may hold values from -0.09375 to 0.09375
- tile_rows: int32 [8, 768], P('layer', 'tile'), may hold values from 0 to 127, as said below
- tile_cols: int32 [8, 768], P('layer', 'tile'), may hold values from 0 to 1, as said below
- tile_count: int32 [8, 64], P('layer', 'tile'), may hold values from 1 to 12, 576 in all within a row
Outputs:
- traces: bfloat16 [8, 2, 32768, 128], P('layer', None, 'tile')
Inputs may be any that keep to these rules, and one draw needn't show every extreme that they name: `tile_rows`: slot i of a layer belongs to tile device d = i // 12; its row block lies among the row blocks held by devices d - 1, d and d + 1, where row block r is held by device r // 2; in every layer some live slot writes to the first row block of the device on its left and some to the last of the device on its right. `tile_cols`: the column block is counted among the 2 row blocks held by the slot's own device. `tile_count`: A device's live slots are its first ones; each layer group has 9 * 64 live slots in all.
All inputs are finite; a program needn't handle non-finite values.
Results may differ from a plain program's by a relative error of at most 0.0095.
Values may be sent and summed in bfloat16 or wider, within the bound.
A program may use at most 64 MiB of HBM per device.

v0:
```python
import jax
import jax.numpy as jnp
from jax import lax
from jax.sharding import PartitionSpec as P


def shifted(block, axis, distance):
    devices = range(lax.axis_size(axis))
    route = [(i - distance, i) for i in devices if i - distance in devices]
    return lax.ppermute(block, axis, route)


def sweep_layer(inbound, source, tiles, tile_row, tile_col, count, place):
    fronts, rows_dev, width = inbound.shape
    half = width // 2
    tile_size = tiles.shape[-1]
    blocks_dev = rows_dev // tile_size
    slot_count = tiles.shape[0]
    blocks = inbound.reshape(fronts, blocks_dev, tile_size, width)
    picked = jnp.take(blocks, tile_col, axis=1)
    swapped = jnp.concatenate([-picked[..., half:], picked[..., :half]], axis=-1)
    stacked = jnp.stack([picked, swapped], axis=2)
    terms = jnp.einsum("tcab,ftcbs->ftas", tiles, stacked, preferred_element_type=jnp.float32)
    active = jnp.arange(slot_count) < count
    target = tile_row - (place - 1) * blocks_dev
    spread = ((target[None, :] == jnp.arange(3 * blocks_dev)[:, None]) & active[None, :]).astype(
        jnp.float32
    )
    window = jnp.einsum("wt,ftas->fwas", spread, terms, precision=lax.Precision.HIGHEST)
    window = window.reshape(fronts, 3, rows_dev, width)
    total = window[:, 1] + source.astype(jnp.float32)
    for offset in (-1, 1):
        outgoing = window[:, 1 + offset].astype(jnp.bfloat16)
        arrived = shifted(outgoing, "tile", offset)
        total = total + arrived.astype(jnp.float32)
    return total.astype(jnp.bfloat16)


def shards(incident, sources, green_tiles, tile_rows, tile_cols, tile_count):
    place = lax.axis_index("tile")
    section = lax.axis_index("layer")
    depth = lax.axis_size("layer")
    tiles = green_tiles[0]
    tile_row = tile_rows[0]
    tile_col = tile_cols[0]
    count = tile_count[0, 0]
    given = sources[0]

    def apply_layer(inbound, source):
        return sweep_layer(inbound, source, tiles, tile_row, tile_col, count, place)

    opening = jnp.where(section == 0, incident, jnp.zeros_like(incident))

    def advance(step, state):
        inbound, result = state
        leaving = apply_layer(inbound, given)
        result = jnp.where(section == step, leaving, result)
        inbound = shifted(leaving, "layer", 1)
        return (inbound, result)

    leftover, result = lax.fori_loop(0, depth, advance, (opening, jnp.zeros_like(incident)))
    return result[None]


def solution(mesh):
    return jax.shard_map(
        shards,
        mesh=mesh,
        in_specs=(
            P(None, "tile", None),
            P("layer", None, "tile", None),
            P("layer", "tile", None, None, None),
            P("layer", "tile"),
            P("layer", "tile"),
            P("layer", "tile"),
        ),
        out_specs=P("layer", None, "tile", None),
        check_vma=False,
    )
```

profile of v0, /device:TPU:217, one launch (start us, length us, event | category | flops | bytes accessed | tf_op | source)
XLA Modules:
  0.0 294.4 jit_solution(14473230811776206770)
XLA Ops:
  0.0 293.7 %while.18 = (s32[]{:T(128)}, bf16[2,512,128]{2,1,0:T(8,128)(2,1)S(1)}, bf16[2,512,128]{2,1,0:T(8,128)(2,1)S(1)}, s32[12]{0:T(128)}, bf16[12,2,256,256]{3,2,1,0:T...) while((s32[]{:T(128)}, ...), condition=%wide.region_1.2_spmd.clone, body=%wide.region_0.1_spmd.clone.sunk | while | flops 870188288 | bytes 61608920 | solution.py:61
  10.7 3.9 %fusion.38 = f32[2,6,256,128]{3,1,2,0:T(8,128)S(1)} fusion(f32[12,2,128,256,1]{2,0,3,1,4:T(8,128)} %copy.21, s32[12]{0:T(128)S(1)} %broadcast_subtract_fusion.2, pred[12]{0:T(512)(128)(4,1)S(1)} %get-tuple-element.374), kind=kOutput, calls=%fused_computation.8.clone.1 | convolution fusion | flops 56623248 | bytes 4718652 | tf_op jit(solution)/shard_map/while/body/eval_jaxpr/wt,ftas->fwas/dot_general | solution.py:29
  15.1 5.0 %collective-permute-start = (bf16[2,512,128]{2,1,0:T(8,128)(2,1)S(1)}, bf16[2,512,128]{2,1,0:T(8,128)(2,1)S(1)}, u32[]{:S(2)}, u32[]{:S(2)}) collective-permute-start(bf16[2,512,128]{2,1,0:T(8,128)(2,1)S(1)} %get-tuple-element.375), channel_id=1, source_target_pairs={{0,1},{1,2},{2,3},{3,4},{4,5},{5,6},{6,7},{7,8},{8,9},{9,10},{10,1... | collective-permute-start | bytes 786440 | tf_op jit(solution)/shard_map/while/body/eval_jaxpr/ppermute | solution.py:10
  23.4 5.6 %collective-permute-done.1 = bf16[2,512,128]{2,1,0:T(8,128)(2,1)S(1)} collective-permute-done((bf16[2,512,128]{2,1,0:T(8,128)(2,1)S(1)}, bf16[2,512,128]{2,1,0:T(8,128)(2,1)S(1)}, u32[]{:S(2)}, u32[]{:S(2)}) %collective-permute-start.1) | collective-permute-done | bytes 262176 | tf_op jit(solution)/shard_map/while/body/eval_jaxpr/ppermute | solution.py:10
  29.2 5.2 %collective-permute-start.2 = (bf16[2,512,128]{2,1,0:T(8,128)(2,1)S(1)}, bf16[2,512,128]{2,1,0:T(8,128)(2,1)S(1)}, u32[]{:S(2)}, u32[]{:S(2)}) collective-permute-start(bf16[2,512,128]{2,1,0:T(8,128)(2,1)S(1)} %get-tuple-element.377), channel_id=1, source_target_pairs={{0,64},{64,128},{128,192},{192,256},{256,320},{320,384},{384,448},... | collective-permute-start | bytes 786440 | tf_op jit(solution)/shard_map/while/body/eval_jaxpr/ppermute | solution.py:10
  52.8 4.2 %collective-permute-start = (bf16[2,512,128]{2,1,0:T(8,128)(2,1)S(1)}, bf16[2,512,128]{2,1,0:T(8,128)(2,1)S(1)}, u32[]{:S(2)}, u32[]{:S(2)}) collective-permute-start(bf16[2,512,128]{2,1,0:T(8,128)(2,1)S(1)} %get-tuple-element.375), channel_id=1, source_target_pairs={{0,1},{1,2},{2,3},{3,4},{4,5},{5,6},{6,7},{7,8},{8,9},{9,10},{10,1... | collective-permute-start | bytes 786440 | tf_op jit(solution)/shard_map/while/body/eval_jaxpr/ppermute | solution.py:10
  60.3 5.6 %collective-permute-done.1 = bf16[2,512,128]{2,1,0:T(8,128)(2,1)S(1)} collective-permute-done((bf16[2,512,128]{2,1,0:T(8,128)(2,1)S(1)}, bf16[2,512,128]{2,1,0:T(8,128)(2,1)S(1)}, u32[]{:S(2)}, u32[]{:S(2)}) %collective-permute-start.1) | collective-permute-done | bytes 262176 | tf_op jit(solution)/shard_map/while/body/eval_jaxpr/ppermute | solution.py:10
  66.1 5.3 %collective-permute-start.2 = (bf16[2,512,128]{2,1,0:T(8,128)(2,1)S(1)}, bf16[2,512,128]{2,1,0:T(8,128)(2,1)S(1)}, u32[]{:S(2)}, u32[]{:S(2)}) collective-permute-start(bf16[2,512,128]{2,1,0:T(8,128)(2,1)S(1)} %get-tuple-element.377), channel_id=1, source_target_pairs={{0,64},{64,128},{128,192},{192,256},{256,320},{320,384},{384,448},... | collective-permute-start | bytes 786440 | tf_op jit(solution)/shard_map/while/body/eval_jaxpr/ppermute | solution.py:10
  85.3 3.9 %fusion.38 = f32[2,6,256,128]{3,1,2,0:T(8,128)S(1)} fusion(f32[12,2,128,256,1]{2,0,3,1,4:T(8,128)} %copy.21, s32[12]{0:T(128)S(1)} %broadcast_subtract_fusion.2, pred[12]{0:T(512)(128)(4,1)S(1)} %get-tuple-element.374), kind=kOutput, calls=%fused_computation.8.clone.1 | convolution fusion | flops 56623248 | bytes 4718652 | tf_op jit(solution)/shard_map/while/body/eval_jaxpr/wt,ftas->fwas/dot_general | solution.py:29
  89.8 4.2 %collective-permute-start = (bf16[2,512,128]{2,1,0:T(8,128)(2,1)S(1)}, bf16[2,512,128]{2,1,0:T(8,128)(2,1)S(1)}, u32[]{:S(2)}, u32[]{:S(2)}) collective-permute-start(bf16[2,512,128]{2,1,0:T(8,128)(2,1)S(1)} %get-tuple-element.375), channel_id=1, source_target_pairs={{0,1},{1,2},{2,3},{3,4},{4,5},{5,6},{6,7},{7,8},{8,9},{9,10},{10,1... | collective-permute-start | bytes 786440 | tf_op jit(solution)/shard_map/while/body/eval_jaxpr/ppermute | solution.py:10
  97.2 5.6 %collective-permute-done.1 = bf16[2,512,128]{2,1,0:T(8,128)(2,1)S(1)} collective-permute-done((bf16[2,512,128]{2,1,0:T(8,128)(2,1)S(1)}, bf16[2,512,128]{2,1,0:T(8,128)(2,1)S(1)}, u32[]{:S(2)}, u32[]{:S(2)}) %collective-permute-start.1) | collective-permute-done | bytes 262176 | tf_op jit(solution)/shard_map/while/body/eval_jaxpr/ppermute | solution.py:10
  103.1 5.3 %collective-permute-start.2 = (bf16[2,512,128]{2,1,0:T(8,128)(2,1)S(1)}, bf16[2,512,128]{2,1,0:T(8,128)(2,1)S(1)}, u32[]{:S(2)}, u32[]{:S(2)}) collective-permute-start(bf16[2,512,128]{2,1,0:T(8,128)(2,1)S(1)} %get-tuple-element.377), channel_id=1, source_target_pairs={{0,64},{64,128},{128,192},{192,256},{256,320},{320,384},{384,448},... | collective-permute-start | bytes 786440 | tf_op jit(solution)/shard_map/while/body/eval_jaxpr/ppermute | solution.py:10
  126.7 4.2 %collective-permute-start = (bf16[2,512,128]{2,1,0:T(8,128)(2,1)S(1)}, bf16[2,512,128]{2,1,0:T(8,128)(2,1)S(1)}, u32[]{:S(2)}, u32[]{:S(2)}) collective-permute-start(bf16[2,512,128]{2,1,0:T(8,128)(2,1)S(1)} %get-tuple-element.375), channel_id=1, source_target_pairs={{0,1},{1,2},{2,3},{3,4},{4,5},{5,6},{6,7},{7,8},{8,9},{9,10},{10,1... | collective-permute-start | bytes 786440 | tf_op jit(solution)/shard_map/while/body/eval_jaxpr/ppermute | solution.py:10
  134.2 5.6 %collective-permute-done.1 = bf16[2,512,128]{2,1,0:T(8,128)(2,1)S(1)} collective-permute-done((bf16[2,512,128]{2,1,0:T(8,128)(2,1)S(1)}, bf16[2,512,128]{2,1,0:T(8,128)(2,1)S(1)}, u32[]{:S(2)}, u32[]{:S(2)}) %collective-permute-start.1) | collective-permute-done | bytes 262176 | tf_op jit(solution)/shard_map/while/body/eval_jaxpr/ppermute | solution.py:10
  140.1 5.3 %collective-permute-start.2 = (bf16[2,512,128]{2,1,0:T(8,128)(2,1)S(1)}, bf16[2,512,128]{2,1,0:T(8,128)(2,1)S(1)}, u32[]{:S(2)}, u32[]{:S(2)}) collective-permute-start(bf16[2,512,128]{2,1,0:T(8,128)(2,1)S(1)} %get-tuple-element.377), channel_id=1, source_target_pairs={{0,64},{64,128},{128,192},{192,256},{256,320},{320,384},{384,448},... | collective-permute-start | bytes 786440 | tf_op jit(solution)/shard_map/while/body/eval_jaxpr/ppermute | solution.py:10
  170.5 5.6 %collective-permute-done.1 = bf16[2,512,128]{2,1,0:T(8,128)(2,1)S(1)} collective-permute-done((bf16[2,512,128]{2,1,0:T(8,128)(2,1)S(1)}, bf16[2,512,128]{2,1,0:T(8,128)(2,1)S(1)}, u32[]{:S(2)}, u32[]{:S(2)}) %collective-permute-start.1) | collective-permute-done | bytes 262176 | tf_op jit(solution)/shard_map/while/body/eval_jaxpr/ppermute | solution.py:10
  176.4 5.3 %collective-permute-start.2 = (bf16[2,512,128]{2,1,0:T(8,128)(2,1)S(1)}, bf16[2,512,128]{2,1,0:T(8,128)(2,1)S(1)}, u32[]{:S(2)}, u32[]{:S(2)}) collective-permute-start(bf16[2,512,128]{2,1,0:T(8,128)(2,1)S(1)} %get-tuple-element.377), channel_id=1, source_target_pairs={{0,64},{64,128},{128,192},{192,256},{256,320},{320,384},{384,448},... | collective-permute-start | bytes 786440 | tf_op jit(solution)/shard_map/while/body/eval_jaxpr/ppermute | solution.py:10
  206.5 5.6 %collective-permute-done.1 = bf16[2,512,128]{2,1,0:T(8,128)(2,1)S(1)} collective-permute-done((bf16[2,512,128]{2,1,0:T(8,128)(2,1)S(1)}, bf16[2,512,128]{2,1,0:T(8,128)(2,1)S(1)}, u32[]{:S(2)}, u32[]{:S(2)}) %collective-permute-start.1) | collective-permute-done | bytes 262176 | tf_op jit(solution)/shard_map/while/body/eval_jaxpr/ppermute | solution.py:10
  212.3 5.3 %collective-permute-start.2 = (bf16[2,512,128]{2,1,0:T(8,128)(2,1)S(1)}, bf16[2,512,128]{2,1,0:T(8,128)(2,1)S(1)}, u32[]{:S(2)}, u32[]{:S(2)}) collective-permute-start(bf16[2,512,128]{2,1,0:T(8,128)(2,1)S(1)} %get-tuple-element.377), channel_id=1, source_target_pairs={{0,64},{64,128},{128,192},{192,256},{256,320},{320,384},{384,448},... | collective-permute-start | bytes 786440 | tf_op jit(solution)/shard_map/while/body/eval_jaxpr/ppermute | solution.py:10
  231.6 3.9 %fusion.38 = f32[2,6,256,128]{3,1,2,0:T(8,128)S(1)} fusion(f32[12,2,128,256,1]{2,0,3,1,4:T(8,128)} %copy.21, s32[12]{0:T(128)S(1)} %broadcast_subtract_fusion.2, pred[12]{0:T(512)(128)(4,1)S(1)} %get-tuple-element.374), kind=kOutput, calls=%fused_computation.8.clone.1 | convolution fusion | flops 56623248 | bytes 4718652 | tf_op jit(solution)/shard_map/while/body/eval_jaxpr/wt,ftas->fwas/dot_general | solution.py:29
  243.0 5.6 %collective-permute-done.1 = bf16[2,512,128]{2,1,0:T(8,128)(2,1)S(1)} collective-permute-done((bf16[2,512,128]{2,1,0:T(8,128)(2,1)S(1)}, bf16[2,512,128]{2,1,0:T(8,128)(2,1)S(1)}, u32[]{:S(2)}, u32[]{:S(2)}) %collective-permute-start.1) | collective-permute-done | bytes 262176 | tf_op jit(solution)/shard_map/while/body/eval_jaxpr/ppermute | solution.py:10
  248.8 5.3 %collective-permute-start.2 = (bf16[2,512,128]{2,1,0:T(8,128)(2,1)S(1)}, bf16[2,512,128]{2,1,0:T(8,128)(2,1)S(1)}, u32[]{:S(2)}, u32[]{:S(2)}) collective-permute-start(bf16[2,512,128]{2,1,0:T(8,128)(2,1)S(1)} %get-tuple-element.377), channel_id=1, source_target_pairs={{0,64},{64,128},{128,192},{192,256},{256,320},{320,384},{384,448},... | collective-permute-start | bytes 786440 | tf_op jit(solution)/shard_map/while/body/eval_jaxpr/ppermute | solution.py:10
  279.2 5.6 %collective-permute-done.1 = bf16[2,512,128]{2,1,0:T(8,128)(2,1)S(1)} collective-permute-done((bf16[2,512,128]{2,1,0:T(8,128)(2,1)S(1)}, bf16[2,512,128]{2,1,0:T(8,128)(2,1)S(1)}, u32[]{:S(2)}, u32[]{:S(2)}) %collective-permute-start.1) | collective-permute-done | bytes 262176 | tf_op jit(solution)/shard_map/while/body/eval_jaxpr/ppermute | solution.py:10
  285.1 5.3 %collective-permute-start.2 = (bf16[2,512,128]{2,1,0:T(8,128)(2,1)S(1)}, bf16[2,512,128]{2,1,0:T(8,128)(2,1)S(1)}, u32[]{:S(2)}, u32[]{:S(2)}) collective-permute-start(bf16[2,512,128]{2,1,0:T(8,128)(2,1)S(1)} %get-tuple-element.377), channel_id=1, source_target_pairs={{0,64},{64,128},{128,192},{192,256},{256,320},{320,384},{384,448},... | collective-permute-start | bytes 786440 | tf_op jit(solution)/shard_map/while/body/eval_jaxpr/ppermute | solution.py:10
  (205 shorter events, 176.6 us)
Async XLA Ops:
  15.1 8.3 %collective-permute-start = (bf16[2,512,128]{2,1,0:T(8,128)(2,1)S(1)}, bf16[2,512,128]{2,1,0:T(8,128)(2,1)S(1)}, u32[]{:S(2)}, u32[]{:S(2)}) collective-permute-start(bf16[2,512,128]{2,1,0:T(8,128)(2,1)S(1)} %get-tuple-element.375), channel_id=1, source_target_pairs={{0,1},{1,2},{2,3},{3,4},{4,5},{5,6},{6,7},{7,8},{8,9},{9,10},{10,1... | collective-permute-start | bytes 786440 | tf_op jit(solution)/shard_map/while/body/eval_jaxpr/ppermute | solution.py:10
  20.1 8.9 %collective-permute-start.1 = (bf16[2,512,128]{2,1,0:T(8,128)(2,1)S(1)}, bf16[2,512,128]{2,1,0:T(8,128)(2,1)S(1)}, u32[]{:S(2)}, u32[]{:S(2)}) collective-permute-start(bf16[2,512,128]{2,1,0:T(8,128)(2,1)S(1)} %get-tuple-element.376), channel_id=1, source_target_pairs={{1,0},{2,1},{3,2},{4,3},{5,4},{6,5},{7,6},{8,7},{9,8},{10,9},{11,1... | collective-permute-start | bytes 786440 | tf_op jit(solution)/shard_map/while/body/eval_jaxpr/ppermute | solution.py:10
  29.2 8.5 %collective-permute-start.2 = (bf16[2,512,128]{2,1,0:T(8,128)(2,1)S(1)}, bf16[2,512,128]{2,1,0:T(8,128)(2,1)S(1)}, u32[]{:S(2)}, u32[]{:S(2)}) collective-permute-start(bf16[2,512,128]{2,1,0:T(8,128)(2,1)S(1)} %get-tuple-element.377), channel_id=1, source_target_pairs={{0,64},{64,128},{128,192},{192,256},{256,320},{320,384},{384,448},... | collective-permute-start | bytes 786440 | tf_op jit(solution)/shard_map/while/body/eval_jaxpr/ppermute | solution.py:10
  52.8 7.5 %collective-permute-start = (bf16[2,512,128]{2,1,0:T(8,128)(2,1)S(1)}, bf16[2,512,128]{2,1,0:T(8,128)(2,1)S(1)}, u32[]{:S(2)}, u32[]{:S(2)}) collective-permute-start(bf16[2,512,128]{2,1,0:T(8,128)(2,1)S(1)} %get-tuple-element.375), channel_id=1, source_target_pairs={{0,1},{1,2},{2,3},{3,4},{4,5},{5,6},{6,7},{7,8},{8,9},{9,10},{10,1... | collective-permute-start | bytes 786440 | tf_op jit(solution)/shard_map/while/body/eval_jaxpr/ppermute | solution.py:10
  57.0 8.9 %collective-permute-start.1 = (bf16[2,512,128]{2,1,0:T(8,128)(2,1)S(1)}, bf16[2,512,128]{2,1,0:T(8,128)(2,1)S(1)}, u32[]{:S(2)}, u32[]{:S(2)}) collective-permute-start(bf16[2,512,128]{2,1,0:T(8,128)(2,1)S(1)} %get-tuple-element.376), channel_id=1, source_target_pairs={{1,0},{2,1},{3,2},{4,3},{5,4},{6,5},{7,6},{8,7},{9,8},{10,9},{11,1... | collective-permute-start | bytes 786440 | tf_op jit(solution)/shard_map/while/body/eval_jaxpr/ppermute | solution.py:10
  66.1 8.6 %collective-permute-start.2 = (bf16[2,512,128]{2,1,0:T(8,128)(2,1)S(1)}, bf16[2,512,128]{2,1,0:T(8,128)(2,1)S(1)}, u32[]{:S(2)}, u32[]{:S(2)}) collective-permute-start(bf16[2,512,128]{2,1,0:T(8,128)(2,1)S(1)} %get-tuple-element.377), channel_id=1, source_target_pairs={{0,64},{64,128},{128,192},{192,256},{256,320},{320,384},{384,448},... | collective-permute-start | bytes 786440 | tf_op jit(solution)/shard_map/while/body/eval_jaxpr/ppermute | solution.py:10
  89.8 7.5 %collective-permute-start = (bf16[2,512,128]{2,1,0:T(8,128)(2,1)S(1)}, bf16[2,512,128]{2,1,0:T(8,128)(2,1)S(1)}, u32[]{:S(2)}, u32[]{:S(2)}) collective-permute-start(bf16[2,512,128]{2,1,0:T(8,128)(2,1)S(1)} %get-tuple-element.375), channel_id=1, source_target_pairs={{0,1},{1,2},{2,3},{3,4},{4,5},{5,6},{6,7},{7,8},{8,9},{9,10},{10,1... | collective-permute-start | bytes 786440 | tf_op jit(solution)/shard_map/while/body/eval_jaxpr/ppermute | solution.py:10
  94.0 8.9 %collective-permute-start.1 = (bf16[2,512,128]{2,1,0:T(8,128)(2,1)S(1)}, bf16[2,512,128]{2,1,0:T(8,128)(2,1)S(1)}, u32[]{:S(2)}, u32[]{:S(2)}) collective-permute-start(bf16[2,512,128]{2,1,0:T(8,128)(2,1)S(1)} %get-tuple-element.376), channel_id=1, source_target_pairs={{1,0},{2,1},{3,2},{4,3},{5,4},{6,5},{7,6},{8,7},{9,8},{10,9},{11,1... | collective-permute-start | bytes 786440 | tf_op jit(solution)/shard_map/while/body/eval_jaxpr/ppermute | solution.py:10
  103.1 8.6 %collective-permute-start.2 = (bf16[2,512,128]{2,1,0:T(8,128)(2,1)S(1)}, bf16[2,512,128]{2,1,0:T(8,128)(2,1)S(1)}, u32[]{:S(2)}, u32[]{:S(2)}) collective-permute-start(bf16[2,512,128]{2,1,0:T(8,128)(2,1)S(1)} %get-tuple-element.377), channel_id=1, source_target_pairs={{0,64},{64,128},{128,192},{192,256},{256,320},{320,384},{384,448},... | collective-permute-start | bytes 786440 | tf_op jit(solution)/shard_map/while/body/eval_jaxpr/ppermute | solution.py:10
  126.7 7.5 %collective-permute-start = (bf16[2,512,128]{2,1,0:T(8,128)(2,1)S(1)}, bf16[2,512,128]{2,1,0:T(8,128)(2,1)S(1)}, u32[]{:S(2)}, u32[]{:S(2)}) collective-permute-start(bf16[2,512,128]{2,1,0:T(8,128)(2,1)S(1)} %get-tuple-element.375), channel_id=1, source_target_pairs={{0,1},{1,2},{2,3},{3,4},{4,5},{5,6},{6,7},{7,8},{8,9},{9,10},{10,1... | collective-permute-start | bytes 786440 | tf_op jit(solution)/shard_map/while/body/eval_jaxpr/ppermute | solution.py:10
  130.9 8.9 %collective-permute-start.1 = (bf16[2,512,128]{2,1,0:T(8,128)(2,1)S(1)}, bf16[2,512,128]{2,1,0:T(8,128)(2,1)S(1)}, u32[]{:S(2)}, u32[]{:S(2)}) collective-permute-start(bf16[2,512,128]{2,1,0:T(8,128)(2,1)S(1)} %get-tuple-element.376), channel_id=1, source_target_pairs={{1,0},{2,1},{3,2},{4,3},{5,4},{6,5},{7,6},{8,7},{9,8},{10,9},{11,1... | collective-permute-start | bytes 786440 | tf_op jit(solution)/shard_map/while/body/eval_jaxpr/ppermute | solution.py:10
  140.1 8.6 %collective-permute-start.2 = (bf16[2,512,128]{2,1,0:T(8,128)(2,1)S(1)}, bf16[2,512,128]{2,1,0:T(8,128)(2,1)S(1)}, u32[]{:S(2)}, u32[]{:S(2)}) collective-permute-start(bf16[2,512,128]{2,1,0:T(8,128)(2,1)S(1)} %get-tuple-element.377), channel_id=1, source_target_pairs={{0,64},{64,128},{128,192},{192,256},{256,320},{320,384},{384,448},... | collective-permute-start | bytes 786440 | tf_op jit(solution)/shard_map/while/body/eval_jaxpr/ppermute | solution.py:10
  163.7 6.8 %collective-permute-start = (bf16[2,512,128]{2,1,0:T(8,128)(2,1)S(1)}, bf16[2,512,128]{2,1,0:T(8,128)(2,1)S(1)}, u32[]{:S(2)}, u32[]{:S(2)}) collective-permute-start(bf16[2,512,128]{2,1,0:T(8,128)(2,1)S(1)} %get-tuple-element.375), channel_id=1, source_target_pairs={{0,1},{1,2},{2,3},{3,4},{4,5},{5,6},{6,7},{7,8},{8,9},{9,10},{10,1... | collective-permute-start | bytes 786440 | tf_op jit(solution)/shard_map/while/body/eval_jaxpr/ppermute | solution.py:10
  167.2 8.9 %collective-permute-start.1 = (bf16[2,512,128]{2,1,0:T(8,128)(2,1)S(1)}, bf16[2,512,128]{2,1,0:T(8,128)(2,1)S(1)}, u32[]{:S(2)}, u32[]{:S(2)}) collective-permute-start(bf16[2,512,128]{2,1,0:T(8,128)(2,1)S(1)} %get-tuple-element.376), channel_id=1, source_target_pairs={{1,0},{2,1},{3,2},{4,3},{5,4},{6,5},{7,6},{8,7},{9,8},{10,9},{11,1... | collective-permute-start | bytes 786440 | tf_op jit(solution)/shard_map/while/body/eval_jaxpr/ppermute | solution.py:10
  176.4 8.6 %collective-permute-start.2 = (bf16[2,512,128]{2,1,0:T(8,128)(2,1)S(1)}, bf16[2,512,128]{2,1,0:T(8,128)(2,1)S(1)}, u32[]{:S(2)}, u32[]{:S(2)}) collective-permute-start(bf16[2,512,128]{2,1,0:T(8,128)(2,1)S(1)} %get-tuple-element.377), channel_id=1, source_target_pairs={{0,64},{64,128},{128,192},{192,256},{256,320},{320,384},{384,448},... | collective-permute-start | bytes 786440 | tf_op jit(solution)/shard_map/while/body/eval_jaxpr/ppermute | solution.py:10
  200.0 6.5 %collective-permute-start = (bf16[2,512,128]{2,1,0:T(8,128)(2,1)S(1)}, bf16[2,512,128]{2,1,0:T(8,128)(2,1)S(1)}, u32[]{:S(2)}, u32[]{:S(2)}) collective-permute-start(bf16[2,512,128]{2,1,0:T(8,128)(2,1)S(1)} %get-tuple-element.375), channel_id=1, source_target_pairs={{0,1},{1,2},{2,3},{3,4},{4,5},{5,6},{6,7},{7,8},{8,9},{9,10},{10,1... | collective-permute-start | bytes 786440 | tf_op jit(solution)/shard_map/while/body/eval_jaxpr/ppermute | solution.py:10
  203.2 8.9 %collective-permute-start.1 = (bf16[2,512,128]{2,1,0:T(8,128)(2,1)S(1)}, bf16[2,512,128]{2,1,0:T(8,128)(2,1)S(1)}, u32[]{:S(2)}, u32[]{:S(2)}) collective-permute-start(bf16[2,512,128]{2,1,0:T(8,128)(2,1)S(1)} %get-tuple-element.376), channel_id=1, source_target_pairs={{1,0},{2,1},{3,2},{4,3},{5,4},{6,5},{7,6},{8,7},{9,8},{10,9},{11,1... | collective-permute-start | bytes 786440 | tf_op jit(solution)/shard_map/while/body/eval_jaxpr/ppermute | solution.py:10
  212.3 8.6 %collective-permute-start.2 = (bf16[2,512,128]{2,1,0:T(8,128)(2,1)S(1)}, bf16[2,512,128]{2,1,0:T(8,128)(2,1)S(1)}, u32[]{:S(2)}, u32[]{:S(2)}) collective-permute-start(bf16[2,512,128]{2,1,0:T(8,128)(2,1)S(1)} %get-tuple-element.377), channel_id=1, source_target_pairs={{0,64},{64,128},{128,192},{192,256},{256,320},{320,384},{384,448},... | collective-permute-start | bytes 786440 | tf_op jit(solution)/shard_map/while/body/eval_jaxpr/ppermute | solution.py:10
  236.0 7.0 %collective-permute-start = (bf16[2,512,128]{2,1,0:T(8,128)(2,1)S(1)}, bf16[2,512,128]{2,1,0:T(8,128)(2,1)S(1)}, u32[]{:S(2)}, u32[]{:S(2)}) collective-permute-start(bf16[2,512,128]{2,1,0:T(8,128)(2,1)S(1)} %get-tuple-element.375), channel_id=1, source_target_pairs={{0,1},{1,2},{2,3},{3,4},{4,5},{5,6},{6,7},{7,8},{8,9},{9,10},{10,1... | collective-permute-start | bytes 786440 | tf_op jit(solution)/shard_map/while/body/eval_jaxpr/ppermute | solution.py:10
  239.7 8.9 %collective-permute-start.1 = (bf16[2,512,128]{2,1,0:T(8,128)(2,1)S(1)}, bf16[2,512,128]{2,1,0:T(8,128)(2,1)S(1)}, u32[]{:S(2)}, u32[]{:S(2)}) collective-permute-start(bf16[2,512,128]{2,1,0:T(8,128)(2,1)S(1)} %get-tuple-element.376), channel_id=1, source_target_pairs={{1,0},{2,1},{3,2},{4,3},{5,4},{6,5},{7,6},{8,7},{9,8},{10,9},{11,1... | collective-permute-start | bytes 786440 | tf_op jit(solution)/shard_map/while/body/eval_jaxpr/ppermute | solution.py:10
  248.8 8.6 %collective-permute-start.2 = (bf16[2,512,128]{2,1,0:T(8,128)(2,1)S(1)}, bf16[2,512,128]{2,1,0:T(8,128)(2,1)S(1)}, u32[]{:S(2)}, u32[]{:S(2)}) collective-permute-start(bf16[2,512,128]{2,1,0:T(8,128)(2,1)S(1)} %get-tuple-element.377), channel_id=1, source_target_pairs={{0,64},{64,128},{128,192},{192,256},{256,320},{320,384},{384,448},... | collective-permute-start | bytes 786440 | tf_op jit(solution)/shard_map/while/body/eval_jaxpr/ppermute | solution.py:10
  272.5 6.8 %collective-permute-start = (bf16[2,512,128]{2,1,0:T(8,128)(2,1)S(1)}, bf16[2,512,128]{2,1,0:T(8,128)(2,1)S(1)}, u32[]{:S(2)}, u32[]{:S(2)}) collective-permute-start(bf16[2,512,128]{2,1,0:T(8,128)(2,1)S(1)} %get-tuple-element.375), channel_id=1, source_target_pairs={{0,1},{1,2},{2,3},{3,4},{4,5},{5,6},{6,7},{7,8},{8,9},{9,10},{10,1... | collective-permute-start | bytes 786440 | tf_op jit(solution)/shard_map/while/body/eval_jaxpr/ppermute | solution.py:10
  276.0 8.9 %collective-permute-start.1 = (bf16[2,512,128]{2,1,0:T(8,128)(2,1)S(1)}, bf16[2,512,128]{2,1,0:T(8,128)(2,1)S(1)}, u32[]{:S(2)}, u32[]{:S(2)}) collective-permute-start(bf16[2,512,128]{2,1,0:T(8,128)(2,1)S(1)} %get-tuple-element.376), channel_id=1, source_target_pairs={{1,0},{2,1},{3,2},{4,3},{5,4},{6,5},{7,6},{8,7},{9,8},{10,9},{11,1... | collective-permute-start | bytes 786440 | tf_op jit(solution)/shard_map/while/body/eval_jaxpr/ppermute | solution.py:10
  285.1 8.6 %collective-permute-start.2 = (bf16[2,512,128]{2,1,0:T(8,128)(2,1)S(1)}, bf16[2,512,128]{2,1,0:T(8,128)(2,1)S(1)}, u32[]{:S(2)}, u32[]{:S(2)}) collective-permute-start(bf16[2,512,128]{2,1,0:T(8,128)(2,1)S(1)} %get-tuple-element.377), channel_id=1, source_target_pairs={{0,64},{64,128},{128,192},{192,256},{256,320},{320,384},{384,448},... | collective-permute-start | bytes 786440 | tf_op jit(solution)/shard_map/while/body/eval_jaxpr/ppermute | solution.py:10
  (25 other events, 147.0 us)
where the time goes:
time: 296 us; the launch traced here: 294 us
  starting transfers between devices  89.1 us (30%)
  waiting for transfers between devices  82.1 us (28%)
  local copies, waits for them, and re-layouts  45.5 us (15%)
  matrix products  42.6 us (14%)
  other arithmetic  33.9 us (11%)
    ppermute x24, starting transfers between devices, shifted(): return lax.ppermute(block, axis, route)  89.1 us
    ppermute x24, waiting for transfers between devices, shifted(): return lax.ppermute(block, axis, route)  82.1 us
    dot_general x8, matrix products, sweep_layer(): jnp.einsum('wt,ftas->fwas', spread, terms, precision=lax.Precision.HIGHEST)  31.5 us
    dot_general x8, local copies, waits for them, and re-layouts, sweep_layer(): jnp.einsum('tcab,ftcbs->ftas', tiles, stacked, preferred_element_type=jnp...  27.1 us
    dot_general x8, matrix products, sweep_layer(): jnp.einsum('tcab,ftcbs->ftas', tiles, stacked, preferred_element_type=jnp...  11.1 us
    and x8, other arithmetic, sweep_layer(): picked = jnp.take(blocks, tile_col, axis=1)  10.5 us
    select_n x24, other arithmetic, sweep_layer(): picked = jnp.take(blocks, tile_col, axis=1)  8.64 us
    while x48, local copies, waits for them, and re-layouts  8.19 us
  transfers between devices with their start and end apart: 24, of which 24 were waited for; matrix products, arithmetic and copies ran while one was open for 0% of the time, Pallas kernels for 0%

commit v1 on v0

v1 whole, which is shorter than its diff:
```python
import functools

import jax
import jax.numpy as jnp
from jax import lax
from jax.experimental import pallas as pl
from jax.experimental.pallas import tpu as pltpu
from jax.sharding import PartitionSpec as P

MESH = pl.DeviceIdType.MESH
VMEM = pl.BlockSpec(memory_space=pltpu.VMEM)
SMEM = pl.BlockSpec(memory_space=pltpu.SMEM)
ANY = pl.BlockSpec(memory_space=pl.ANY)
CHUNKS = 16
LAG = 3
F32 = jnp.float32
BF16 = jnp.bfloat16


def beside(place):
    odd = lax.rem(place, 2)
    return place - 1 + 2 * odd, place + 1 - 2 * odd


def prepare(rows_ref, cols_ref, count_ref, tiles_ref, incident_ref, source_ref,
            dense_ref, opening_ref, given_ref, held, extra, total, sem, extra_sem):
    slots, block = tiles_ref.shape[1], tiles_ref.shape[3]
    place = lax.axis_index("tile")
    across, partner = beside(place)
    live = count_ref[0, 0]
    pairs = []
    for part, owner in enumerate((across, partner, place)):
        for r in range(2):
            for c in range(2):
                wanted = owner * 2 + r
                number, first = jnp.int32(0), jnp.int32(0)
                for i in reversed(range(slots)):
                    match = (i < live) & (rows_ref[0, i] == wanted) & (cols_ref[0, i] == c)
                    number = number + match.astype(jnp.int32)
                    first = jnp.where(match, i, first)
                p = len(pairs)
                pltpu.make_async_copy(tiles_ref.at[0, first], held.at[p], sem.at[p]).start()
                pairs.append((part * 2 * block + r * block, c * block, wanted, c, number))
    chunks, width, _ = opening_ref.shape
    each, half = chunks // 2, width // 2
    for array, out in ((incident_ref, opening_ref), (source_ref.at[0], given_ref)):
        for f in range(2):
            turned = array[f].astype(F32).T
            mid = turned.shape[0] // 2
            for j in range(each):
                piece = jnp.concatenate(
                    [turned[j * half:(j + 1) * half], turned[mid + j * half:mid + (j + 1) * half]], axis=0)
                out[f * each + j] = piece.astype(BF16)
    depth = 2 * block
    for p, (at, under, wanted, c, number) in enumerate(pairs):
        pltpu.make_async_copy(tiles_ref.at[0, 0], held.at[p], sem.at[p]).wait()

        @pl.when(number == 0)
        def _():
            for s in range(2):
                dense_ref[s * depth + under:s * depth + under + block, at:at + block] = jnp.zeros((block, block), BF16)

        @pl.when(number == 1)
        def _():
            for s in range(2):
                dense_ref[s * depth + under:s * depth + under + block, at:at + block] = held[p, s].T

        @pl.when(number > 1)
        def _():
            total[...] = jnp.zeros_like(total)

            def add(i, _):
                @pl.when((i < live) & (rows_ref[0, i] == wanted) & (cols_ref[0, i] == c))
                def _():
                    copy = pltpu.make_async_copy(tiles_ref.at[0, i], extra, extra_sem)
                    copy.start()
                    copy.wait()
                    total[...] += extra[...].astype(F32)
                return 0

            lax.fori_loop(0, slots, add, 0)
            for s in range(2):
                dense_ref[s * depth + under:s * depth + under + block, at:at + block] = total[s].T.astype(BF16)


def sweep(layers, places, dense_ref, opening_ref, given_ref, out_ref,
          own_in, ext_in, side_in, mate_in, own_out, ext_out, mate_out, kept,
          own_s, ext_s, side_s, mate_s, own_r, ext_r, side_r, mate_r):
    chunks, width, rows = opening_ref.shape
    half = width // 2
    layer, place = lax.axis_index("layer"), lax.axis_index("tile")
    across, partner = beside(place)
    has = (across >= 0) & (across < places)
    above, below = layer > 0, layer < layers - 1
    barrier = pltpu.get_barrier_semaphore()

    def hello(l, t):
        pl.semaphore_signal(barrier, inc=1, device_id=(l, t), device_id_type=MESH)

    hello(layer, partner)

    @pl.when(has)
    def _():
        hello(layer, across)

    @pl.when(above)
    def _():
        hello(layer - 1, place)

    @pl.when(above & has)
    def _():
        hello(layer - 1, across)

    @pl.when(jnp.logical_not(above))
    def _():
        own_in[...] = opening_ref[...]

    @pl.when(jnp.logical_not(above & has))
    def _():
        ext_in[...] = jnp.zeros_like(ext_in)

    @pl.when(jnp.logical_not(has))
    def _():
        side_in[...] = jnp.zeros_like(side_in)

    beyond = has.astype(jnp.int32)
    pl.semaphore_wait(barrier, (1 + beyond) * (1 + below.astype(jnp.int32)))

    def send(src, dst, s, r, c, l, t):
        return pltpu.make_async_remote_copy(
            src_ref=src.at[c], dst_ref=dst.at[c], send_sem=s.at[c], recv_sem=r.at[c],
            device_id=(l, t), device_id_type=MESH)

    def to_mate(c):
        return send(mate_out, mate_in, mate_s, mate_r, c, layer, partner)

    def to_side(c):
        return send(ext_out, side_in, side_s, side_r, c, layer, across)

    def to_own(c):
        return send(own_out, own_in, own_s, own_r, c, layer + 1, place)

    def to_ext(c):
        return send(ext_out, ext_in, ext_s, ext_r, c, layer + 1, across)

    def multiply(c):
        @pl.when(above)
        def _():
            to_own(c).wait_recv()

        @pl.when(above & has)
        def _():
            to_ext(c).wait_recv()

        u = (own_in[c].astype(F32) + ext_in[c].astype(F32)).astype(BF16).astype(F32)
        turned = jnp.concatenate([-u[half:], u[:half]], axis=0)
        stacked = jnp.concatenate([u, turned], axis=1).astype(BF16)

        def part(k):
            return jnp.dot(stacked, dense_ref[:, k * rows:(k + 1) * rows], preferred_element_type=F32)

        ext_out[c] = part(0).astype(BF16)

        @pl.when(below & has)
        def _():
            to_ext(c).start()

        @pl.when(has)
        def _():
            to_side(c).start()

        mate_out[c] = part(1).astype(BF16)
        to_mate(c).start()
        kept[c] = part(2) + given_ref[c].astype(F32)

    def combine(c):
        to_mate(c).wait_recv()
        y = kept[c] + mate_in[c].astype(F32)
        kept[c] = y
        own_out[c] = y.astype(BF16)

        @pl.when(below)
        def _():
            to_own(c).start()

    def finish(c):
        @pl.when(has)
        def _():
            to_side(c).wait_recv()

        out_ref[c] = (kept[c] + side_in[c].astype(F32)).astype(BF16)

    def step(t, _):
        @pl.when(t < chunks)
        def _():
            multiply(t)

        @pl.when((t >= 1) & (t < chunks + 1))
        def _():
            combine(t - 1)

        @pl.when(t >= LAG)
        def _():
            finish(t - LAG)
        return 0

    lax.fori_loop(0, chunks + LAG, step, 0)

    def drain(c, _):
        to_mate(c).wait_send()

        @pl.when(has)
        def _():
            to_side(c).wait_send()

        @pl.when(below)
        def _():
            to_own(c).wait_send()

        @pl.when(below & has)
        def _():
            to_ext(c).wait_send()
        return 0

    lax.fori_loop(0, chunks, drain, 0)


def restore(trace_ref, out_ref, scratch):
    chunks, width, _ = trace_ref.shape
    each, half = chunks // 2, width // 2
    mid = scratch.shape[1] // 2
    for f in range(2):
        for j in range(each):
            piece = trace_ref[f * each + j].astype(F32)
            scratch[f, j * half:(j + 1) * half] = piece[:half]
            scratch[f, mid + j * half:mid + (j + 1) * half] = piece[half:]
        out_ref[0, f] = scratch[f].T.astype(BF16)


def shards(layers, places, incident, sources, green_tiles, tile_rows, tile_cols, tile_count):
    fronts, rows, columns = incident.shape
    slots, _, block, _ = green_tiles.shape[1:]
    width = fronts * columns // CHUNKS
    chunked = jax.ShapeDtypeStruct((CHUNKS, width, rows), BF16)
    dense, opening, given = pl.pallas_call(
        prepare,
        out_shape=(jax.ShapeDtypeStruct((4 * block, 3 * rows), BF16), chunked, chunked),
        in_specs=[SMEM, SMEM, SMEM, ANY, VMEM, VMEM],
        out_specs=(VMEM, VMEM, VMEM),
        scratch_shapes=[
            pltpu.VMEM((12, 2, block, block), BF16),
            pltpu.VMEM((2, block, block), BF16),
            pltpu.VMEM((2, block, block), F32),
            pltpu.SemaphoreType.DMA((12,)),
            pltpu.SemaphoreType.DMA,
        ],
        compiler_params=pltpu.CompilerParams(vmem_limit_bytes=24 * 2**20),
    )(tile_rows, tile_cols, tile_count, green_tiles, incident, sources)
    buffer = pltpu.VMEM((CHUNKS, width, rows), BF16)
    trace = pl.pallas_call(
        functools.partial(sweep, layers, places),
        out_shape=chunked,
        in_specs=[VMEM, VMEM, VMEM],
        out_specs=VMEM,
        scratch_shapes=[buffer] * 7
        + [pltpu.VMEM((CHUNKS, width, rows), F32)]
        + [pltpu.SemaphoreType.DMA((CHUNKS,))] * 8,
        compiler_params=pltpu.CompilerParams(
            collective_id=0, has_side_effects=True, vmem_limit_bytes=24 * 2**20),
    )(dense, opening, given)
    return pl.pallas_call(
        restore,
        out_shape=jax.ShapeDtypeStruct((1, fronts, rows, columns), BF16),
        in_specs=[VMEM],
        out_specs=VMEM,
        scratch_shapes=[pltpu.VMEM((fronts, columns, rows), F32)],
    )(trace)


def solution(mesh):
    return jax.shard_map(
        functools.partial(shards, mesh.shape["layer"], mesh.shape["tile"]),
        mesh=mesh,
        in_specs=(
            P(None, "tile", None),
            P("layer", None, "tile", None),
            P("layer", "tile", None, None, None),
            P("layer", "tile"),
            P("layer", "tile"),
            P("layer", "tile"),
        ),
        out_specs=P("layer", None, "tile", None),
        check_vma=False,
    )
```

time: 296 us -> 61.7 us (0.21)
  the two profiles are of different devices: /device:TPU:217 before, /device:TPU:454 now
where the time goes in v1:
time: 61.7 us; the launch traced here: 61.4 us
  Pallas kernels  54.9 us (89%)
  local copies, waits for them, and re-layouts  5.79 us (9%)
  between operations  0.69 us (1%)
    pallas_call x1, Pallas kernels, shards(): pl.pallas_call(functools.partial(sweep, layers, places), out_shape=chunke...  50.2 us
    unnamed x12, local copies, waits for them, and re-layouts  5.79 us
    pallas_call x1, Pallas kernels, shards(): pl.pallas_call(prepare, out_shape=(jax.ShapeDtypeStruct((4 * block, 3 * r...  2.96 us
    pallas_call x1, Pallas kernels, shards(): pl.pallas_call(restore, out_shape=jax.ShapeDtypeStruct((1, fronts, rows,...  1.79 us

profile of v1, /device:TPU:454, one launch (start us, length us, event | category | flops | bytes accessed | tf_op | source)
XLA Modules:
  0.0 61.4 jit_solution(5193363908580987824)
XLA Ops:
  0.7 0.0 copy-start
  0.7 1.9 %copy-done = bf16[1,12,2,256,256]{4,3,2,1,0:T(8,128)(2,1)S(1)} copy-done((bf16[1,12,2,256,256]{4,3,2,1,0:T(8,128)(2,1)S(1)}, bf16[1,12,2,256,256]{4,3,2,1,0:T(8,128)(2,1)}, u32[]{:S(2)}) %copy-start) | copy-done | bytes 3145752
  2.5 0.0 copy-start.2
  2.5 0.9 %copy-done.2 = bf16[2,512,128]{2,1,0:T(8,128)(2,1)S(1)} copy-done((bf16[2,512,128]{2,1,0:T(8,128)(2,1)S(1)}, bf16[2,512,128]{2,1,0:T(8,128)(2,1)}, u32[]{:S(2)}) %copy-start.2) | copy-done | bytes 262168
  3.5 0.0 copy-start.3
  3.5 0.9 %copy-done.3 = bf16[1,2,512,128]{3,2,1,0:T(8,128)(2,1)S(1)} copy-done((bf16[1,2,512,128]{3,2,1,0:T(8,128)(2,1)S(1)}, bf16[1,2,512,128]{3,2,1,0:T(8,128)(2,1)}, u32[]{:S(2)}) %copy-start.3) | copy-done | bytes 262168
  4.4 0.0 copy-start.4
  4.4 0.7 %copy-done.4 = s32[1,12]{1,0:T(1,128)S(1)} copy-done((s32[1,12]{1,0:T(1,128)S(1)}, s32[1,12]{1,0:T(1,128)}, u32[]{:S(2)}) %copy-start.4) | copy-done | bytes 72
  5.1 0.0 copy-start.5
  5.1 0.7 %copy-done.5 = s32[1,12]{1,0:T(1,128)S(1)} copy-done((s32[1,12]{1,0:T(1,128)S(1)}, s32[1,12]{1,0:T(1,128)}, u32[]{:S(2)}) %copy-start.5) | copy-done | bytes 72
  5.8 3.0 %shard_map.64 = (bf16[1024,1536]{1,0:T(8,128)(2,1)S(1)}, bf16[16,16,512]{2,1,0:T(8,128)(2,1)S(1)}, bf16[16,16,512]{2,1,0:T(8,128)(2,1)S(1)}) custom-call(s32[1,12]{1,0:T(1,128)S(1)} %copy-done.4, s32[1,12]{1,0:T(1,128)S(1)} %copy-done.5, s32[1,1]{1,0:T(1,128)S(6)} %copy.7.count_ref, bf16[1,12,2,256,256]{4,3,2,1,0:T(8,128)(2,1)S(1)} %copy-done, ...), custom_call_target="tpu_custom_call" | custom-call | tf_op jit(solution)/shard_map/pallas_call | solution.py:245
  8.7 50.2 %shard_map.65.trace_ref = bf16[16,16,512]{2,1,0:T(8,128)(2,1)S(1)} custom-call(bf16[1024,1536]{1,0:T(8,128)(2,1)S(1)} %get-tuple-element.8.dense_ref, bf16[16,16,512]{2,1,0:T(8,128)(2,1)S(1)} %get-tuple-element.9.opening_ref, bf16[16,16,512]{2,1,0:T(8,128)(2,1)S(1)} %get-tuple-element.10.given_ref), custom_call_target="tpu_custom_call" | custom-call | tf_op jit(solution)/shard_map/pallas_call | solution.py:260
  58.9 0.0 copy-start.1
  58.9 0.7 %copy-done.1 = bf16[16,16,512]{2,1,0:T(8,128)(2,1)} copy-done((bf16[16,16,512]{2,1,0:T(8,128)(2,1)}, bf16[16,16,512]{2,1,0:T(8,128)(2,1)S(1)}, u32[]{:S(2)}) %copy-start.1) | copy-done | bytes 262168
  59.6 1.8 %shard_map.66 = bf16[1,2,512,128]{3,2,1,0:T(8,128)(2,1)} custom-call(bf16[16,16,512]{2,1,0:T(8,128)(2,1)} %copy-done.1), custom_call_target="tpu_custom_call" | custom-call | tf_op jit(solution)/shard_map/pallas_call | solution.py:271
Async XLA Ops:
  0.7 1.9 %copy-start = (bf16[1,12,2,256,256]{4,3,2,1,0:T(8,128)(2,1)S(1)}, bf16[1,12,2,256,256]{4,3,2,1,0:T(8,128)(2,1)}, u32[]{:S(2)}) copy-start(bf16[1,12,2,256,256]{4,3,2,1,0:T(8,128)(2,1)} %tiles_ref.1) | copy-start | bytes 9437188
  2.5 0.9 %copy-start.2 = (bf16[2,512,128]{2,1,0:T(8,128)(2,1)S(1)}, bf16[2,512,128]{2,1,0:T(8,128)(2,1)}, u32[]{:S(2)}) copy-start(bf16[2,512,128]{2,1,0:T(8,128)(2,1)} %incident_ref.1) | copy-start | bytes 786436
  3.5 0.9 %copy-start.3 = (bf16[1,2,512,128]{3,2,1,0:T(8,128)(2,1)S(1)}, bf16[1,2,512,128]{3,2,1,0:T(8,128)(2,1)}, u32[]{:S(2)}) copy-start(bf16[1,2,512,128]{3,2,1,0:T(8,128)(2,1)} %source_ref.1) | copy-start | bytes 786436
  4.4 0.7 %copy-start.4 = (s32[1,12]{1,0:T(1,128)S(1)}, s32[1,12]{1,0:T(1,128)}, u32[]{:S(2)}) copy-start(s32[1,12]{1,0:T(1,128)} %rows_ref.1) | copy-start | bytes 148
  5.1 0.7 %copy-start.5 = (s32[1,12]{1,0:T(1,128)S(1)}, s32[1,12]{1,0:T(1,128)}, u32[]{:S(2)}) copy-start(s32[1,12]{1,0:T(1,128)} %cols_ref.1) | copy-start | bytes 148
  58.9 0.7 %copy-start.1 = (bf16[16,16,512]{2,1,0:T(8,128)(2,1)}, bf16[16,16,512]{2,1,0:T(8,128)(2,1)S(1)}, u32[]{:S(2)}) copy-start(bf16[16,16,512]{2,1,0:T(8,128)(2,1)S(1)} %shard_map.65.trace_ref) | copy-start | bytes 786436

commit v2 on v0

v2 whole, which is shorter than its diff:
```python
import functools

import jax
import jax.numpy as jnp
from jax import lax
from jax.experimental import pallas as pl
from jax.experimental.pallas import tpu as pltpu
from jax.sharding import PartitionSpec as P

MESH = pl.DeviceIdType.MESH
VMEM = pl.BlockSpec(memory_space=pltpu.VMEM)
HBM = pl.BlockSpec(memory_space=pltpu.HBM)
CHUNKS = 16
LAG = 6
F32 = jnp.float32
BF16 = jnp.bfloat16


def sweep(layers, places, rows_hbm, cols_hbm, count_hbm, tiles_hbm, incident_hbm, source_hbm, out_ref,
          rows_ref, cols_ref, count_ref, tiles_ref, incident_ref, source_ref, dense, given, result,
          own_in, ext_in, side_in, mate_in, own_out, ext_out, mate_out, kept,
          index_sem, array_sem, tile_sem,
          own_s, ext_s, side_s, mate_s, own_r, ext_r, side_r, mate_r):
    slots, block = tiles_ref.shape[0], tiles_ref.shape[2]
    chunks, width, rows = own_in.shape
    each, half = chunks // 2, width // 2
    layer, place = lax.axis_index("layer"), lax.axis_index("tile")
    odd = lax.rem(place, 2)
    partner = place + 1 - 2 * odd
    beyond = place - 1 + 2 * odd
    inner = (beyond >= 0) & (beyond < places)
    across = jnp.where(inner, beyond, partner)
    aside = jnp.where(inner, 0, chunks)
    beside_edge = (partner == 0) | (partner == places - 1)
    above, below = layer > 0, layer < layers - 1

    index_copies = [
        pltpu.make_async_copy(src, dst, index_sem.at[i])
        for i, (src, dst) in enumerate(((rows_hbm, rows_ref), (cols_hbm, cols_ref), (count_hbm, count_ref)))
    ]
    array_copies = [
        pltpu.make_async_copy(incident_hbm, incident_ref, array_sem.at[0]),
        pltpu.make_async_copy(source_hbm.at[0], source_ref, array_sem.at[1]),
    ]
    tile_copies = [pltpu.make_async_copy(tiles_hbm.at[0, i], tiles_ref.at[i], tile_sem.at[i]) for i in range(slots)]
    for copy in index_copies + array_copies[:1] + tile_copies + array_copies[1:]:
        copy.start()

    barrier = pltpu.get_barrier_semaphore()

    def hello(l, t):
        pl.semaphore_signal(barrier, inc=1, device_id=(l, t), device_id_type=MESH)

    hello(layer, partner)

    @pl.when(inner)
    def _():
        hello(layer, across)

    @pl.when(above)
    def _():
        hello(layer - 1, place)

    @pl.when(above & inner)
    def _():
        hello(layer - 1, across)

    @pl.when(above & beside_edge)
    def _():
        hello(layer - 1, partner)

    dense[slots] = jnp.zeros(dense.shape[1:], BF16)

    for copy in index_copies:
        copy.wait()
    live = count_ref[0, 0]
    keys = []
    for i in range(slots):
        row = rows_ref[0, i]
        owner = row // 2
        part = jnp.where(owner == beyond, 0, jnp.where(owner == partner, 1, 2))
        keys.append(jnp.where(i < live, part * 4 + (row - 2 * owner) * 2 + cols_ref[0, i], 16 + i))
    before = []
    for i in range(slots):
        found = jnp.int32(slots)
        for j in range(i):
            found = jnp.where(keys[j] == keys[i], j, found)
        before.append(found)
    last = []
    for p in range(12):
        found = jnp.int32(slots)
        for i in range(slots):
            found = jnp.where(keys[i] == p, i, found)
        last.append(found)

    array_copies[0].wait()

    @pl.when(jnp.logical_not(above))
    def _():
        for f in range(2):
            turned = incident_ref[f].astype(F32).T.reshape(2, each, half, rows)
            for j in range(each):
                own_in[f * each + j] = turned[:, j].reshape(width, rows).astype(BF16)

    @pl.when(jnp.logical_not(above & inner))
    def _():
        ext_in[:chunks] = jnp.zeros((chunks, width, rows), BF16)

    @pl.when(jnp.logical_not(inner))
    def _():
        side_in[:chunks] = jnp.zeros((chunks, width, rows), BF16)

    for i in range(slots):
        tile_copies[i].wait()
        for s in range(2):
            dense[i, s] = (tiles_ref[i, s].T.astype(F32) + dense[before[i], s].astype(F32)).astype(BF16)

    array_copies[1].wait()
    for f in range(2):
        given[f] = source_ref[f].astype(F32).T.reshape(2, each, half, rows)

    pl.semaphore_wait(barrier, 1 + inner.astype(jnp.int32) + 2 * below.astype(jnp.int32))

    def send(src, dst, s, r, c, l, t, to=0):
        return pltpu.make_async_remote_copy(
            src_ref=src.at[c], dst_ref=dst.at[c + to], send_sem=s.at[c], recv_sem=r.at[c + to],
            device_id=(l, t), device_id_type=MESH)

    def to_mate(c):
        return send(mate_out, mate_in, mate_s, mate_r, c, layer, partner)

    def to_side(c):
        return send(ext_out, side_in, side_s, side_r, c, layer, across, aside)

    def to_own(c):
        return send(own_out, own_in, own_s, own_r, c, layer + 1, place)

    def to_ext(c):
        return send(ext_out, ext_in, ext_s, ext_r, c, layer + 1, across, aside)

    def arrived(dst, s, r, c):
        send(dst, dst, s, r, c, layer, partner).wait_recv()

    def multiply(c, onward):
        @pl.when(above)
        def _():
            to_own(c).wait_recv()

        @pl.when(above & inner)
        def _():
            arrived(ext_in, ext_s, ext_r, c)

        u = (own_in[c].astype(F32) + ext_in[c].astype(F32)).astype(BF16).astype(F32)
        sides = (u.astype(BF16), jnp.concatenate([-u[half:], u[:half]], axis=0).astype(BF16))

        def part(k):
            outs = []
            for r in range(2):
                total = None
                for b in range(2):
                    for s in range(2):
                        term = jnp.dot(sides[s][:, b * block:(b + 1) * block],
                                       dense[last[4 * k + 2 * r + b], s], preferred_element_type=F32)
                        total = term if total is None else total + term
                outs.append(total)
            return jnp.concatenate(outs, axis=1)

        ext_out[c] = part(0).astype(BF16)
        if onward:
            to_ext(c).start()
        mate_out[c] = part(1).astype(BF16)
        to_mate(c).start()
        to_side(c).start()
        source = given[c // each, :, c % each].reshape(width, rows)
        kept[c] = part(2) + source

    def combine(c, onward):
        to_mate(c).wait_recv()
        y = kept[c] + mate_in[c].astype(F32)
        kept[c] = y
        if onward:
            own_out[c] = y.astype(BF16)
            to_own(c).start()

    def finish(c):
        @pl.when(inner)
        def _():
            arrived(side_in, side_s, side_r, c)

        result[c // each, :, c % each] = (kept[c] + side_in[c].astype(F32)).reshape(2, half, rows)

    def pipeline(onward):
        multiply(0, onward)

        def step(t, _):
            multiply(t, onward)
            combine(t - 1, onward)

            @pl.when(t >= LAG)
            def _():
                finish(t - LAG)
            return 0

        lax.fori_loop(1, chunks, step, 0)
        combine(chunks - 1, onward)

    @pl.when(below)
    def _():
        pipeline(True)

    @pl.when(jnp.logical_not(below))
    def _():
        pipeline(False)

    def leave(f):
        out_ref[0, f] = result[f].reshape(2 * each * half, rows).T.astype(BF16)

    leave(0)

    def last_step(c, _):
        finish(c)
        return 0

    lax.fori_loop(chunks - LAG, chunks, last_step, 0)
    leave(1)

    def drain(c, _):
        to_mate(c).wait_send()
        to_side(c).wait_send()

        @pl.when(below)
        def _():
            to_own(c).wait_send()
            to_ext(c).wait_send()

        @pl.when(beside_edge)
        def _():
            arrived(side_in, side_s, side_r, chunks + c)

        @pl.when(above & beside_edge)
        def _():
            arrived(ext_in, ext_s, ext_r, chunks + c)
        return 0

    lax.fori_loop(0, chunks, drain, 0)


def shards(layers, places, incident, sources, green_tiles, tile_rows, tile_cols, tile_count):
    fronts, rows, columns = incident.shape
    slots, _, block, _ = green_tiles.shape[1:]
    width = fronts * columns // CHUNKS
    buffer = pltpu.VMEM((CHUNKS, width, rows), BF16)
    double = pltpu.VMEM((2 * CHUNKS, width, rows), BF16)
    split = pltpu.VMEM((fronts, 2, CHUNKS // 2, width // 2, rows), F32)
    return pl.pallas_call(
        functools.partial(sweep, layers, places),
        out_shape=jax.ShapeDtypeStruct((1, fronts, rows, columns), BF16),
        in_specs=[HBM] * 6,
        out_specs=VMEM,
        scratch_shapes=[
            pltpu.SMEM(tile_rows.shape, jnp.int32),
            pltpu.SMEM(tile_cols.shape, jnp.int32),
            pltpu.SMEM(tile_count.shape, jnp.int32),
            pltpu.VMEM((slots, 2, block, block), BF16),
            pltpu.VMEM((fronts, rows, columns), BF16),
            pltpu.VMEM((fronts, rows, columns), BF16),
            pltpu.VMEM((slots + 1, 2, block, block), BF16),
            split,
            split,
        ]
        + [buffer, double, double] + [buffer] * 4
        + [pltpu.VMEM((CHUNKS, width, rows), F32)]
        + [pltpu.SemaphoreType.DMA((3,)), pltpu.SemaphoreType.DMA((2,)), pltpu.SemaphoreType.DMA((slots,))]
        + [pltpu.SemaphoreType.DMA((CHUNKS,))] * 4
        + [pltpu.SemaphoreType.DMA((2 * CHUNKS,))] * 4,
        compiler_params=pltpu.CompilerParams(
            collective_id=0, has_side_effects=True, vmem_limit_bytes=60 * 2**20),
    )(tile_rows, tile_cols, tile_count, green_tiles, incident, sources)


def solution(mesh):
    return jax.shard_map(
        functools.partial(shards, mesh.shape["layer"], mesh.shape["tile"]),
        mesh=mesh,
        in_specs=(
            P(None, "tile", None),
            P("layer", None, "tile", None),
            P("layer", "tile", None, None, None),
            P("layer", "tile"),
            P("layer", "tile"),
            P("layer", "tile"),
        ),
        out_specs=P("layer", None, "tile", None),
        check_vma=False,
    )
```

time: 296 us -> 56.9 us (0.19)
  the two profiles are of different devices: /device:TPU:217 before, /device:TPU:449 now
where the time goes in v2:
time: 56.9 us; the launch traced here: 56.6 us
  Pallas kernels  54.3 us (95%)
  local copies, waits for them, and re-layouts  1.67 us (3%)
  between operations  0.66 us (1%)
    pallas_call x1, Pallas kernels, shards(): pl.pallas_call(functools.partial(sweep, layers, places), out_shape=jax.Sh...  54.3 us
    unnamed x1, local copies, waits for them, and re-layouts  1.67 us

profile of v2, /device:TPU:449, one launch (start us, length us, event | category | flops | bytes accessed | tf_op | source)
XLA Modules:
  0.0 56.6 jit_solution(11536235899648592465)
XLA Ops:
  0.7 54.3 %shard_map.64 = bf16[1,2,512,128]{3,2,1,0:T(8,128)(2,1)} custom-call(s32[1,12]{1,0:T(1,128)} %rows_hbm.1, s32[1,12]{1,0:T(1,128)} %cols_hbm.1, s32[1,1]{1,0:T(1,128)S(6)} %copy.8.count_hbm, bf16[1,12,2,256,256]{4,3,2,1,0:T(8,128)(2,1)} %tiles_hbm.1, bf16[2,512,128]{2,1,0:T(8,128)(2,1)} %incident_hbm.1, bf16[1,2,512,128]{3,2,1,0:T(8,128)(2,1)} %source_hbm.1), custom_call_target="tpu_custom_call" | custom-call | tf_op jit(solution)/shard_map/pallas_call | solution.py:255
  55.0 1.7 %copy.9 = bf16[1,2,512,128]{3,2,1,0:T(8,128)(2,1)} copy(bf16[1,2,512,128]{3,2,1,0:T(8,128)(2,1)} %shard_map.64) | data formatting | bytes 524288

commit v3 on v2

--- a/solution.py
+++ b/solution.py
@@ -12,6 +12,7 @@
 HBM = pl.BlockSpec(memory_space=pltpu.HBM)
 CHUNKS = 16
 LAG = 6
+GROUP = 3
 F32 = jnp.float32
 BF16 = jnp.bfloat16
 
@@ -29,9 +30,6 @@
     partner = place + 1 - 2 * odd
     beyond = place - 1 + 2 * odd
     inner = (beyond >= 0) & (beyond < places)
-    across = jnp.where(inner, beyond, partner)
-    aside = jnp.where(inner, 0, chunks)
-    beside_edge = (partner == 0) | (partner == places - 1)
     above, below = layer > 0, layer < layers - 1
 
     index_copies = [
@@ -42,7 +40,10 @@
         pltpu.make_async_copy(incident_hbm, incident_ref, array_sem.at[0]),
         pltpu.make_async_copy(source_hbm.at[0], source_ref, array_sem.at[1]),
     ]
-    tile_copies = [pltpu.make_async_copy(tiles_hbm.at[0, i], tiles_ref.at[i], tile_sem.at[i]) for i in range(slots)]
+    tile_copies = [
+        pltpu.make_async_copy(tiles_hbm.at[0, pl.ds(i, GROUP)], tiles_ref.at[pl.ds(i, GROUP)], tile_sem.at[i])
+        for i in range(0, slots, GROUP)
+    ]
     for copy in index_copies + array_copies[:1] + tile_copies + array_copies[1:]:
         copy.start()
 
@@ -55,7 +56,7 @@
 
     @pl.when(inner)
     def _():
-        hello(layer, across)
+        hello(layer, beyond)
 
     @pl.when(above)
     def _():
@@ -63,11 +64,7 @@
 
     @pl.when(above & inner)
     def _():
-        hello(layer - 1, across)
-
-    @pl.when(above & beside_edge)
-    def _():
-        hello(layer - 1, partner)
+        hello(layer - 1, beyond)
 
     dense[slots] = jnp.zeros(dense.shape[1:], BF16)
 
@@ -93,53 +90,54 @@
             found = jnp.where(keys[i] == p, i, found)
         last.append(found)
 
-    array_copies[0].wait()
-
-    @pl.when(jnp.logical_not(above))
-    def _():
-        for f in range(2):
+    def turn_incident(f):
+        @pl.when(jnp.logical_not(above))
+        def _():
             turned = incident_ref[f].astype(F32).T.reshape(2, each, half, rows)
             for j in range(each):
                 own_in[f * each + j] = turned[:, j].reshape(width, rows).astype(BF16)
 
+    array_copies[0].wait()
+    turn_incident(0)
+
     @pl.when(jnp.logical_not(above & inner))
     def _():
-        ext_in[:chunks] = jnp.zeros((chunks, width, rows), BF16)
+        ext_in[...] = jnp.zeros_like(ext_in)
 
     @pl.when(jnp.logical_not(inner))
     def _():
-        side_in[:chunks] = jnp.zeros((chunks, width, rows), BF16)
+        side_in[...] = jnp.zeros_like(ext_in)
 
     for i in range(slots):
-        tile_copies[i].wait()
+        if i % GROUP == 0:
+            tile_copies[i // GROUP].wait()
         for s in range(2):
             dense[i, s] = (tiles_ref[i, s].T.astype(F32) + dense[before[i], s].astype(F32)).astype(BF16)
 
-    array_copies[1].wait()
-    for f in range(2):
-        given[f] = source_ref[f].astype(F32).T.reshape(2, each, half, rows)
-
-    pl.semaphore_wait(barrier, 1 + inner.astype(jnp.int32) + 2 * below.astype(jnp.int32))
-
-    def send(src, dst, s, r, c, l, t, to=0):
+    def turn_sources():
+        array_copies[1].wait()
+        turn_incident(1)
+        for f in range(2):
+            given[f] = source_ref[f].astype(F32).T.reshape(2, each, half, rows)
+
+    pl.semaphore_wait(barrier, (1 + inner.astype(jnp.int32)) * (1 + below.astype(jnp.int32)))
+
+    def send(src, dst, s, r, c, l, t):
         return pltpu.make_async_remote_copy(
-            src_ref=src.at[c], dst_ref=dst.at[c + to], send_sem=s.at[c], recv_sem=r.at[c + to],
+            src_ref=src.at[c], dst_ref=dst.at[c], send_sem=s.at[c], recv_sem=r.at[c],
             device_id=(l, t), device_id_type=MESH)
 
     def to_mate(c):
         return send(mate_out, mate_in, mate_s, mate_r, c, layer, partner)
 
     def to_side(c):
-        return send(ext_out, side_in, side_s, side_r, c, layer, across, aside)
+        return send(ext_out, side_in, side_s, side_r, c, layer, beyond)
 
     def to_own(c):
         return send(own_out, own_in, own_s, own_r, c, layer + 1, place)
 
     def to_ext(c):
-        return send(ext_out, ext_in, ext_s, ext_r, c, layer + 1, across, aside)
-
-    def arrived(dst, s, r, c):
-        send(dst, dst, s, r, c, layer, partner).wait_recv()
+        return send(ext_out, ext_in, ext_s, ext_r, c, layer + 1, beyond)
 
     def multiply(c, onward):
         @pl.when(above)
@@ -148,7 +146,7 @@
 
         @pl.when(above & inner)
         def _():
-            arrived(ext_in, ext_s, ext_r, c)
+            to_ext(c).wait_recv()
 
         u = (own_in[c].astype(F32) + ext_in[c].astype(F32)).astype(BF16).astype(F32)
         sides = (u.astype(BF16), jnp.concatenate([-u[half:], u[:half]], axis=0).astype(BF16))
@@ -165,18 +163,26 @@
                 outs.append(total)
             return jnp.concatenate(outs, axis=1)
 
+        def exchange():
+            mate_out[c] = part(1).astype(BF16)
+            to_mate(c).start()
+
+        if onward:
+            exchange()
         ext_out[c] = part(0).astype(BF16)
-        if onward:
-            to_ext(c).start()
-        mate_out[c] = part(1).astype(BF16)
-        to_mate(c).start()
-        to_side(c).start()
-        source = given[c // each, :, c % each].reshape(width, rows)
-        kept[c] = part(2) + source
-
-    def combine(c, onward):
-        to_mate(c).wait_recv()
-        y = kept[c] + mate_in[c].astype(F32)
+
+        @pl.when(inner)
+        def _():
+            if onward:
+                to_ext(c).start()
+            to_side(c).start()
+
+        if not onward:
+            exchange()
+        return lambda: part(2)
+
+    def combine(c, own, onward):
+        y = own + mate_in[c].astype(F32) + given[c // each, :, c % each].reshape(width, rows)
         kept[c] = y
         if onward:
             own_out[c] = y.astype(BF16)
@@ -185,16 +191,19 @@
     def finish(c):
         @pl.when(inner)
         def _():
-            arrived(side_in, side_s, side_r, c)
+            to_side(c).wait_recv()
 
         result[c // each, :, c % each] = (kept[c] + side_in[c].astype(F32)).reshape(2, half, rows)
 
     def pipeline(onward):
-        multiply(0, onward)
+        kept[0] = multiply(0, onward)()
+        turn_sources()
 
         def step(t, _):
-            multiply(t, onward)
-            combine(t - 1, onward)
+            own = multiply(t, onward)
+            to_mate(t - 1).wait_recv()
+            combine(t - 1, kept[t - 1], onward)
+            kept[t] = own()
 
             @pl.when(t >= LAG)
             def _():
@@ -202,7 +211,8 @@
             return 0
 
         lax.fori_loop(1, chunks, step, 0)
-        combine(chunks - 1, onward)
+        to_mate(chunks - 1).wait_recv()
+        combine(chunks - 1, kept[chunks - 1], onward)
 
     @pl.when(below)
     def _():
@@ -226,20 +236,18 @@
 
     def drain(c, _):
         to_mate(c).wait_send()
-        to_side(c).wait_send()
+
+        @pl.when(inner)
+        def _():
+            to_side(c).wait_send()
 
         @pl.when(below)
         def _():
             to_own(c).wait_send()
+
+        @pl.when(below & inner)
+        def _():
             to_ext(c).wait_send()
-
-        @pl.when(beside_edge)
-        def _():
-            arrived(side_in, side_s, side_r, chunks + c)
-
-        @pl.when(above & beside_edge)
-        def _():
-            arrived(ext_in, ext_s, ext_r, chunks + c)
         return 0
 
     lax.fori_loop(0, chunks, drain, 0)
@@ -250,11 +258,10 @@
     slots, _, block, _ = green_tiles.shape[1:]
     width = fronts * columns // CHUNKS
     buffer = pltpu.VMEM((CHUNKS, width, rows), BF16)
-    double = pltpu.VMEM((2 * CHUNKS, width, rows), BF16)
     split = pltpu.VMEM((fronts, 2, CHUNKS // 2, width // 2, rows), F32)
     return pl.pallas_call(
         functools.partial(sweep, layers, places),
-        out_shape=jax.ShapeDtypeStruct((1, fronts, rows, columns), BF16),
+        out_shape=pltpu.VMEM((1, fronts, rows, columns), BF16),
         in_specs=[HBM] * 6,
         out_specs=VMEM,
         scratch_shapes=[
@@ -268,14 +275,20 @@
             split,
             split,
         ]
-        + [buffer, double, double] + [buffer] * 4
+        + [buffer] * 7
         + [pltpu.VMEM((CHUNKS, width, rows), F32)]
         + [pltpu.SemaphoreType.DMA((3,)), pltpu.SemaphoreType.DMA((2,)), pltpu.SemaphoreType.DMA((slots,))]
-        + [pltpu.SemaphoreType.DMA((CHUNKS,))] * 4
-        + [pltpu.SemaphoreType.DMA((2 * CHUNKS,))] * 4,
+        + [pltpu.SemaphoreType.DMA((CHUNKS,))] * 8,
         compiler_params=pltpu.CompilerParams(
-            collective_id=0, has_side_effects=True, vmem_limit_bytes=60 * 2**20),
-    )(tile_rows, tile_cols, tile_count, green_tiles, incident, sources)
+            collective_id=0, has_side_effects=True, vmem_limit_bytes=32 * 2**20),
+    )(
+        pltpu.with_memory_space_constraint(tile_rows, pltpu.HBM),
+        pltpu.with_memory_space_constraint(tile_cols, pltpu.HBM),
+        tile_count,
+        pltpu.with_memory_space_constraint(green_tiles, pltpu.HBM),
+        pltpu.with_memory_space_constraint(incident, pltpu.HBM),
+        pltpu.with_memory_space_constraint(sources, pltpu.HBM),
+    )
 
 
 def solution(mesh):

time: 56.9 us -> 50.7 us (0.89)
  Pallas kernels: 54.3 us -> 49.2 us
  local copies, waits for them, and re-layouts: 1.67 us -> 0.71 us
    pallas_call x1, Pallas kernels: 54.3 us -> 49.2 us  [shards(): pl.pallas_call(functools.partial(sweep, layers, places), out_shape=pltpu....]
    unnamed x1, local copies, waits for them, and re-layouts: 1.67 us -> 0.71 us
where the time goes in v3:
time: 50.7 us; the launch traced here: 50.6 us
  Pallas kernels  49.2 us (97%)
  local copies, waits for them, and re-layouts  0.71 us (1%)
  between operations  0.66 us (1%)
    pallas_call x1, Pallas kernels, shards(): pl.pallas_call(functools.partial(sweep, layers, places), out_shape=pltpu....  49.2 us

profile of v3, /device:TPU:449, one launch (start us, length us, event | category | flops | bytes accessed | tf_op | source)
XLA Modules:
  0.0 50.6 jit_solution(9033025836868977768)
XLA Ops:
  0.7 49.2 %shard_map.64 = bf16[1,2,512,128]{3,2,1,0:T(8,128)(2,1)S(1)} custom-call(s32[1,12]{1,0:T(1,128)} %rows_hbm.1, s32[1,12]{1,0:T(1,128)} %cols_hbm.1, s32[1,1]{1,0:T(1,128)S(6)} %copy.9.count_hbm, bf16[1,12,2,256,256]{4,3,2,1,0:T(8,128)(2,1)} %tiles_hbm.1, bf16[2,512,128]{2,1,0:T(8,128)(2,1)} %incident_hbm.1, bf16[1,2,512,128]{3,2,1,0:T(8,128)(2,1)} %source_hbm.1), custom_call_target="tpu_custom_call" | custom-call | tf_op jit(solution)/shard_map/pallas_call | solution.py:262
  49.9 0.7 %copy.8 = bf16[1,2,512,128]{3,2,1,0:T(8,128)(2,1)} copy(bf16[1,2,512,128]{3,2,1,0:T(8,128)(2,1)S(1)} %shard_map.64) | data formatting | bytes 524288

commit v4 on v3

--- a/solution.py
+++ b/solution.py
@@ -13,6 +13,7 @@
 CHUNKS = 16
 LAG = 6
 GROUP = 3
+ROW = 16
 F32 = jnp.float32
 BF16 = jnp.bfloat16
 
@@ -30,6 +31,8 @@
     partner = place + 1 - 2 * odd
     beyond = place - 1 + 2 * odd
     inner = (beyond >= 0) & (beyond < places)
+    outer = jnp.logical_not(inner)
+    far = inner & ((lax.rem(place, ROW) == 0) | (lax.rem(place, ROW) == ROW - 1))
     above, below = layer > 0, layer < layers - 1
 
     index_copies = [
@@ -104,10 +107,6 @@
     def _():
         ext_in[...] = jnp.zeros_like(ext_in)
 
-    @pl.when(jnp.logical_not(inner))
-    def _():
-        side_in[...] = jnp.zeros_like(ext_in)
-
     for i in range(slots):
         if i % GROUP == 0:
             tile_copies[i // GROUP].wait()
@@ -139,14 +138,12 @@
     def to_ext(c):
         return send(ext_out, ext_in, ext_s, ext_r, c, layer + 1, beyond)
 
-    def multiply(c, onward):
+    def multiply(c, onward, kind):
         @pl.when(above)
         def _():
             to_own(c).wait_recv()
-
-        @pl.when(above & inner)
-        def _():
-            to_ext(c).wait_recv()
+            if kind != "outer":
+                to_ext(c).wait_recv()
 
         u = (own_in[c].astype(F32) + ext_in[c].astype(F32)).astype(BF16).astype(F32)
         sides = (u.astype(BF16), jnp.concatenate([-u[half:], u[:half]], axis=0).astype(BF16))
@@ -167,71 +164,76 @@
             mate_out[c] = part(1).astype(BF16)
             to_mate(c).start()
 
-        if onward:
-            exchange()
-        ext_out[c] = part(0).astype(BF16)
-
-        @pl.when(inner)
-        def _():
+        def reach():
+            ext_out[c] = part(0).astype(BF16)
             if onward:
                 to_ext(c).start()
             to_side(c).start()
 
-        if not onward:
+        if kind == "far":
+            reach()
             exchange()
+        else:
+            exchange()
+            if kind != "outer":
+                reach()
         return lambda: part(2)
 
-    def combine(c, own, onward):
-        y = own + mate_in[c].astype(F32) + given[c // each, :, c % each].reshape(width, rows)
-        kept[c] = y
+    def combine(c, own, kind, onward):
+        y = own + given[c // each, :, c % each].reshape(width, rows) + mate_in[c].astype(F32)
+        if kind == "outer":
+            result[c // each, :, c % each] = y.reshape(2, half, rows)
+        else:
+            kept[c] = y
         if onward:
             own_out[c] = y.astype(BF16)
             to_own(c).start()
 
     def finish(c):
-        @pl.when(inner)
-        def _():
-            to_side(c).wait_recv()
-
+        to_side(c).wait_recv()
         result[c // each, :, c % each] = (kept[c] + side_in[c].astype(F32)).reshape(2, half, rows)
 
-    def pipeline(onward):
-        kept[0] = multiply(0, onward)()
+    def pipeline(onward, kind):
+        kept[0] = multiply(0, onward, kind)()
         turn_sources()
 
         def step(t, _):
-            own = multiply(t, onward)
+            own = multiply(t, onward, kind)
             to_mate(t - 1).wait_recv()
-            combine(t - 1, kept[t - 1], onward)
+            combine(t - 1, kept[t - 1], kind, onward)
             kept[t] = own()
-
-            @pl.when(t >= LAG)
-            def _():
-                finish(t - LAG)
+            if kind != "outer":
+                @pl.when(t >= LAG)
+                def _():
+                    finish(t - LAG)
             return 0
 
         lax.fori_loop(1, chunks, step, 0)
         to_mate(chunks - 1).wait_recv()
-        combine(chunks - 1, kept[chunks - 1], onward)
-
-    @pl.when(below)
-    def _():
-        pipeline(True)
-
-    @pl.when(jnp.logical_not(below))
-    def _():
-        pipeline(False)
+        combine(chunks - 1, kept[chunks - 1], kind, onward)
+        leave(0)
+
+        def last_step(c, _):
+            finish(c)
+            return 0
+
+        if kind != "outer":
+            lax.fori_loop(chunks - LAG, chunks, last_step, 0)
 
     def leave(f):
         out_ref[0, f] = result[f].reshape(2 * each * half, rows).T.astype(BF16)
 
-    leave(0)
-
-    def last_step(c, _):
-        finish(c)
-        return 0
-
-    lax.fori_loop(chunks - LAG, chunks, last_step, 0)
+    plain = jnp.logical_not(far | outer)
+    for onward, mine in ((True, below), (False, jnp.logical_not(below))):
+        for kind, such in (("plain", plain), ("far", far), ("outer", outer)):
+            if onward or kind in ("far", "outer"):
+                if not onward and kind == "far":
+                    such = inner
+
+                @pl.when(mine & such)
+                def _():
+                    pipeline(onward, kind)
+
     leave(1)
 
     def drain(c, _):

time: 50.7 us -> 49 us (0.966)
  Pallas kernels: 49.2 us -> 47.4 us
    pallas_call x1, Pallas kernels: 49.2 us -> 47.4 us  [shards(): pl.pallas_call(functools.partial(sweep, layers, places), out_shape=pltpu....]
where the time goes in v4:
time: 49 us; the launch traced here: 48.8 us
  Pallas kernels  47.4 us (97%)
  local copies, waits for them, and re-layouts  0.71 us (1%)
  between operations  0.66 us (1%)
    pallas_call x1, Pallas kernels, shards(): pl.pallas_call(functools.partial(sweep, layers, places), out_shape=pltpu....  47.4 us

profile of v4, /device:TPU:449, one launch (start us, length us, event | category | flops | bytes accessed | tf_op | source)
XLA Modules:
  0.0 48.8 jit_solution(16706798642939196953)
XLA Ops:
  0.7 47.4 %shard_map.64 = bf16[1,2,512,128]{3,2,1,0:T(8,128)(2,1)S(1)} custom-call(s32[1,12]{1,0:T(1,128)} %rows_hbm.1, s32[1,12]{1,0:T(1,128)} %cols_hbm.1, s32[1,1]{1,0:T(1,128)S(6)} %copy.9.count_hbm, bf16[1,12,2,256,256]{4,3,2,1,0:T(8,128)(2,1)} %tiles_hbm.1, bf16[2,512,128]{2,1,0:T(8,128)(2,1)} %incident_hbm.1, bf16[1,2,512,128]{3,2,1,0:T(8,128)(2,1)} %source_hbm.1), custom_call_target="tpu_custom_call" | custom-call | tf_op jit(solution)/shard_map/pallas_call | solution.py:264
  48.1 0.7 %copy.8 = bf16[1,2,512,128]{3,2,1,0:T(8,128)(2,1)} copy(bf16[1,2,512,128]{3,2,1,0:T(8,128)(2,1)S(1)} %shard_map.64) | data formatting | bytes 524288

commit v5 on v4

--- a/solution.py
+++ b/solution.py
@@ -47,9 +47,6 @@
         pltpu.make_async_copy(tiles_hbm.at[0, pl.ds(i, GROUP)], tiles_ref.at[pl.ds(i, GROUP)], tile_sem.at[i])
         for i in range(0, slots, GROUP)
     ]
-    for copy in index_copies + array_copies[:1] + tile_copies + array_copies[1:]:
-        copy.start()
-
     barrier = pltpu.get_barrier_semaphore()
 
     def hello(l, t):
@@ -68,6 +65,9 @@
     @pl.when(above & inner)
     def _():
         hello(layer - 1, beyond)
+
+    for copy in index_copies + array_copies[:1] + tile_copies + array_copies[1:]:
+        copy.start()
 
     dense[slots] = jnp.zeros(dense.shape[1:], BF16)
 

time: 49 us -> 48.9 us (level)
  no operation moved by 1% of the time
where the time goes in v5:
time: 48.9 us; the launch traced here: 48.7 us
  Pallas kernels  47.3 us (97%)
  local copies, waits for them, and re-layouts  0.71 us (1%)
  between operations  0.66 us (1%)
    pallas_call x1, Pallas kernels, shards(): pl.pallas_call(functools.partial(sweep, layers, places), out_shape=pltpu....  47.3 us

profile of v5, /device:TPU:449, one launch (start us, length us, event | category | flops | bytes accessed | tf_op | source)
XLA Modules:
  0.0 48.7 jit_solution(10129897895027880570)
XLA Ops:
  0.7 47.3 %shard_map.64 = bf16[1,2,512,128]{3,2,1,0:T(8,128)(2,1)S(1)} custom-call(s32[1,12]{1,0:T(1,128)} %rows_hbm.1, s32[1,12]{1,0:T(1,128)} %cols_hbm.1, s32[1,1]{1,0:T(1,128)S(6)} %copy.9.count_hbm, bf16[1,12,2,256,256]{4,3,2,1,0:T(8,128)(2,1)} %tiles_hbm.1, bf16[2,512,128]{2,1,0:T(8,128)(2,1)} %incident_hbm.1, bf16[1,2,512,128]{3,2,1,0:T(8,128)(2,1)} %source_hbm.1), custom_call_target="tpu_custom_call" | custom-call | tf_op jit(solution)/shard_map/pallas_call | solution.py:264
  48.0 0.7 %copy.8 = bf16[1,2,512,128]{3,2,1,0:T(8,128)(2,1)} copy(bf16[1,2,512,128]{3,2,1,0:T(8,128)(2,1)S(1)} %shard_map.64) | data formatting | bytes 524288

commit v6 on v5

--- a/solution.py
+++ b/solution.py
@@ -138,6 +138,11 @@
     def to_ext(c):
         return send(ext_out, ext_in, ext_s, ext_r, c, layer + 1, beyond)
 
+    def depart(c, onward):
+        if onward:
+            to_ext(c).start()
+        to_side(c).start()
+
     def multiply(c, onward, kind):
         @pl.when(above)
         def _():
@@ -166,9 +171,8 @@
 
         def reach():
             ext_out[c] = part(0).astype(BF16)
-            if onward:
-                to_ext(c).start()
-            to_side(c).start()
+            if kind != "plain":
+                depart(c, onward)
 
         if kind == "far":
             reach()
@@ -194,13 +198,18 @@
         result[c // each, :, c % each] = (kept[c] + side_in[c].astype(F32)).reshape(2, half, rows)
 
     def pipeline(onward, kind):
-        kept[0] = multiply(0, onward, kind)()
+        own = multiply(0, onward, kind)
+        if kind == "plain":
+            depart(0, onward)
+        kept[0] = own()
         turn_sources()
 
         def step(t, _):
             own = multiply(t, onward, kind)
             to_mate(t - 1).wait_recv()
             combine(t - 1, kept[t - 1], kind, onward)
+            if kind == "plain":
+                depart(t, onward)
             kept[t] = own()
             if kind != "outer":
                 @pl.when(t >= LAG)

time: 48.9 us -> 49.2 us (level)
  no operation moved by 1% of the time
where the time goes in v6:
time: 49.2 us; the launch traced here: 49.1 us
  Pallas kernels  47.7 us (97%)
  local copies, waits for them, and re-layouts  0.71 us (1%)
  between operations  0.66 us (1%)
    pallas_call x1, Pallas kernels, shards(): pl.pallas_call(functools.partial(sweep, layers, places), out_shape=pltpu....  47.7 us

profile of v6, /device:TPU:449, one launch (start us, length us, event | category | flops | bytes accessed | tf_op | source)
XLA Modules:
  0.0 49.1 jit_solution(12675419836104281621)
XLA Ops:
  0.7 47.7 %shard_map.64 = bf16[1,2,512,128]{3,2,1,0:T(8,128)(2,1)S(1)} custom-call(s32[1,12]{1,0:T(1,128)} %rows_hbm.1, s32[1,12]{1,0:T(1,128)} %cols_hbm.1, s32[1,1]{1,0:T(1,128)S(6)} %copy.9.count_hbm, bf16[1,12,2,256,256]{4,3,2,1,0:T(8,128)(2,1)} %tiles_hbm.1, bf16[2,512,128]{2,1,0:T(8,128)(2,1)} %incident_hbm.1, bf16[1,2,512,128]{3,2,1,0:T(8,128)(2,1)} %source_hbm.1), custom_call_target="tpu_custom_call" | custom-call | tf_op jit(solution)/shard_map/pallas_call | solution.py:273
  48.4 0.7 %copy.8 = bf16[1,2,512,128]{3,2,1,0:T(8,128)(2,1)} copy(bf16[1,2,512,128]{3,2,1,0:T(8,128)(2,1)S(1)} %shard_map.64) | data formatting | bytes 524288
